TPU v7x, 32 devices: a whole 2x2x4 slice. The times are simulated.
32 devices in a mesh: grp: 4 (over z), seq: 8 (over y, x, core).
Axes of the slice: x: 2, y: 2, z: 4, core: 2. Of those that a mesh axis runs over, the one named last changes fastest.
Arguments:
- tokens: bfloat16 [32768, 512], P(('grp', 'seq')), may hold values from -6 to 6
- norm_gain1: float32 [512], replicated, may hold values from 0.5 to 1.5
- w_xz: bfloat16 [512, 2048], replicated, may hold values from -0.25 to 0.25
- w_bc: bfloat16 [512, 256], replicated, may hold values from -0.0234375 to 0.0234375
- w_dt: bfloat16 [512, 16], replicated, may hold values from -0.25 to 0.25
- dt_bias: float32 [16], replicated, may hold values from -1 to 1
- decay_rate: float32 [16], replicated, may hold values from 1.5258789e-06 to 0.08
- curve_jump: float32 [32768], P(('grp', 'seq')), may hold values from 0 to 1.4
- skip_gain: float32 [16], replicated, may hold values from 0.3 to 1
- norm_gain2: float32 [1024], replicated, may hold values from 0.5 to 1.5
- w_out: bfloat16 [1024, 512], replicated, may hold values from -0.1875 to 0.1875
- norm_gain3: float32 [512], replicated, may hold values from 0.5 to 1.5
- w_q: bfloat16 [512, 1024], replicated, may hold values from -15.909903 to 15.909903
- w_kv: bfloat16 [512, 2048], replicated, may hold values from -0.25 to 0.25
- w_o: bfloat16 [1024, 512], replicated, may hold values from -0.1875 to 0.1875
- nbr_owner: int32 [512, 2], P(('grp', 'seq')), may hold values from 0 to 7, all different within a row; in each aligned block of 16 rows (0 to 15, 16 to 31, ...) at most 4 rows name the same one
- nbr_block: int32 [512, 2], P(('grp', 'seq')), may hold values from 0 to 15
Outputs:
- layer_out: bfloat16 [32768, 512], P(('grp', 'seq'))
Inputs may be any that keep to these rules, and one draw needn't show every extreme that they name: `nbr_owner`: no two slots of one block name the same owner; among the lists of one device's 16 blocks no owner is named more than 4 times, and in every draw some device names one owner exactly 4 times.
All inputs are finite; a program needn't handle non-finite values.
Results may differ from a plain program's by a relative error of at most 0.023.
Values may be sent and summed in bfloat16 or wider, within the bound.
A program may use at most 192 MiB of HBM per device.

v0:
```python
import functools
import math

import jax
import jax.numpy as jnp
from jax import lax
from jax.experimental import pallas as pl
from jax.experimental.pallas import tpu as pltpu
from jax.sharding import PartitionSpec as P

H = 16
P_SIZE = 64
NS = 128
INNER = 1024
CH = 128
BL = 64
KN = 2
PAIRS = INNER // 128
ROWS = 16
EPS = 1e-05
VMEM_LIMIT = 56 * 1024 * 1024
MESH = pl.DeviceIdType.MESH
F32 = jnp.float32
BF16 = jnp.bfloat16


def dot(a, b):
    return jnp.dot(a, b, preferred_element_type=F32)


def dot_nt(a, b):
    return lax.dot_general(a, b, (((1,), (1,)), ((), ())), preferred_element_type=F32)


def dot_tn(a, b):
    return lax.dot_general(a, b, (((0,), (0,)), ((), ())), preferred_element_type=F32)


def rms_rows(values, weights):
    floats = values.astype(F32)
    scale = lax.rsqrt(jnp.mean(floats * floats, axis=-1, keepdims=True) + EPS)
    return (floats * scale * weights).astype(BF16)


def split3(values):
    high = values.astype(BF16)
    rest = values - high.astype(F32)
    middle = rest.astype(BF16)
    low = (rest - middle.astype(F32)).astype(BF16)
    return jnp.concatenate([high, middle, low], axis=0)


def head_spread():
    head = lax.broadcasted_iota(jnp.int32, (3 * H, INNER), 0) % H
    lane = lax.broadcasted_iota(jnp.int32, (3 * H, INNER), 1) // P_SIZE
    return (head == lane).astype(BF16)


def local_kernel(
    tokens_ref, gain_ref, w_xz_ref, w_bc_ref, w_dt_ref, bias_ref, rate_ref, jump_ref,
    xz_ref, maps_ref, intra_ref, reach_ref, state_ref, factor_ref, total_ref, final_ref,
    carried, product,
):
    step = pl.program_id(0)
    chunks = tokens_ref.shape[0] // CH

    @pl.when(step == 0)
    def _():
        carried[...] = jnp.zeros_like(carried)
        product[...] = jnp.ones_like(product)

    normed = rms_rows(tokens_ref[...], gain_ref[...])
    xz_ref[...] = dot(normed, w_xz_ref[...]).astype(BF16)
    maps_ref[...] = dot(normed, w_bc_ref[...]).astype(BF16)
    steps_t = jax.nn.softplus(
        lax.dot_general(
            w_dt_ref[...], normed, (((0,), (1,)), ((), ())), preferred_element_type=F32
        )
        + bias_ref[...]
    )
    row = lax.broadcasted_iota(jnp.int32, (CH, CH), 0)
    col = lax.broadcasted_iota(jnp.int32, (CH, CH), 1)
    lower = row >= col
    upto = (row <= col).astype(F32)
    spread = head_spread()
    first_half = lax.broadcasted_iota(jnp.int32, (CH, 128), 1) < P_SIZE
    for c in range(chunks):
        rows = slice(c * CH, (c + 1) * CH)
        u_t = steps_t[:, rows]
        decay_t = -(rate_ref[...] * u_t + jump_ref[c])
        run_t = jnp.dot(decay_t, upto, precision=lax.Precision.HIGHEST, preferred_element_type=F32)
        run = jnp.concatenate([run_t, jnp.zeros((CH - H, CH), F32)], axis=0).T
        reach_t = jnp.exp(run_t)
        tail_t = jnp.exp(run_t[:, CH - 1 :] - run_t) * u_t
        reach_ref[:, rows] = reach_t
        tail_weight = dot_tn(split3(tail_t), spread)
        last = dot_tn(split3(reach_t[:, CH - 8 :]), spread)[7:8]
        b = maps_ref[rows, :NS]
        cmap = maps_ref[rows, NS:]
        crossing = dot_nt(cmap, b)
        for p in range(PAIRS):
            lanes = slice(p * 128, (p + 1) * 128)
            x = xz_ref[rows, lanes]
            parts = []
            for h in (2 * p, 2 * p + 1):
                gap = run[:, h : h + 1] - run_t[h : h + 1, :]
                weight = jnp.exp(jnp.where(lower, gap, -1e30))
                parts.append((crossing * weight * u_t[h : h + 1, :]).astype(BF16))
            zero = jnp.zeros_like(x)
            stacked = jnp.concatenate(
                [jnp.where(first_half, x, zero), jnp.where(first_half, zero, x)], axis=0
            )
            intra_ref[rows, lanes] = dot(jnp.concatenate(parts, axis=1), stacked)
        state_ref[c] = carried[...]
        factor_ref[c] = jnp.broadcast_to(product[...], (8, INNER))
        tail = (tail_weight * xz_ref[rows, :INNER].astype(F32)).astype(BF16)
        carried[...] = last * carried[...] + dot_tn(b, tail)
        product[...] = product[...] * last

    @pl.when(step == pl.num_programs(0) - 1)
    def _():
        final_ref[...] = carried[...].astype(BF16)
        for i in range(8):
            total_ref[i : i + 1, :] = product[:, i * 128 : (i + 1) * 128]


def local_part(tokens, gain, w_xz, w_bc, w_dt, bias, rate, jump):
    count = tokens.shape[0]
    tile = 2 * CH
    chunks = count // CH
    whole = lambda *shape: pl.BlockSpec(shape, lambda i: (0,) * len(shape))
    return pl.pallas_call(
        local_kernel,
        grid=(count // tile,),
        in_specs=[
            pl.BlockSpec((tile, 512), lambda i: (i, 0)),
            whole(1, 512),
            whole(512, 2 * INNER),
            whole(512, 2 * NS),
            whole(512, H),
            whole(H, 1),
            whole(H, 1),
            pl.BlockSpec((2, 1, CH), lambda i: (i, 0, 0)),
        ],
        out_specs=[
            pl.BlockSpec((tile, 2 * INNER), lambda i: (i, 0)),
            pl.BlockSpec((tile, 2 * NS), lambda i: (i, 0)),
            pl.BlockSpec((tile, INNER), lambda i: (i, 0)),
            pl.BlockSpec((H, tile), lambda i: (0, i)),
            pl.BlockSpec((2, NS, INNER), lambda i: (i, 0, 0)),
            pl.BlockSpec((2, 8, INNER), lambda i: (i, 0, 0)),
            whole(8, 128),
            whole(NS, INNER),
        ],
        out_shape=[
            jax.ShapeDtypeStruct((count, 2 * INNER), BF16),
            jax.ShapeDtypeStruct((count, 2 * NS), BF16),
            jax.ShapeDtypeStruct((count, INNER), F32),
            jax.ShapeDtypeStruct((H, count), F32),
            jax.ShapeDtypeStruct((chunks, NS, INNER), F32),
            jax.ShapeDtypeStruct((chunks, 8, INNER), F32),
            jax.ShapeDtypeStruct((8, 128), F32),
            jax.ShapeDtypeStruct((NS, INNER), BF16),
        ],
        scratch_shapes=[pltpu.VMEM((NS, INNER), F32), pltpu.VMEM((1, INNER), F32)],
        compiler_params=pltpu.CompilerParams(vmem_limit_bytes=VMEM_LIMIT),
        name="local_part",
    )(tokens, gain, w_xz, w_bc, w_dt, bias, rate, jump)


def greet(n_grp, n_seq, grp, seq):
    barrier = pltpu.get_barrier_semaphore()
    for d in range(1, n_seq):
        pl.semaphore_signal(
            barrier, inc=1, device_id=(grp, lax.rem(seq + d, n_seq)), device_id_type=MESH
        )
    for d in range(1, n_grp):
        pl.semaphore_signal(
            barrier, inc=1, device_id=(lax.rem(grp + d, n_grp), seq), device_id_type=MESH
        )
    pl.semaphore_wait(barrier, n_seq + n_grp - 2)


def prefix_kernel(
    n_grp, n_seq, state_ref, total_ref, wanted_ref, before_ref, asked_ref,
    parts, factors, sums, group_factor, shares, group_sum, my_factor, factor_row,
    send1, recv1, send2, recv2, send3, recv3, send4, recv4, send5, recv5, send6, recv6,
):
    grp, seq = lax.axis_index("grp"), lax.axis_index("seq")
    width = parts.shape[-1]
    greet(n_grp, n_seq, grp, seq)
    peers = [lax.rem(seq + d, n_seq) for d in range(n_seq)]
    origins = [lax.rem(seq + n_seq - d, n_seq) for d in range(n_seq)]
    layers = [lax.rem(grp + d, n_grp) for d in range(n_grp)]

    def across(src, dst, send, recv, d):
        return pltpu.make_async_remote_copy(
            src_ref=src, dst_ref=dst, send_sem=send.at[d], recv_sem=recv.at[d],
            device_id=(grp, peers[d]), device_id_type=MESH,
        )

    def along(src, dst, send, recv, d):
        return pltpu.make_async_remote_copy(
            src_ref=src, dst_ref=dst, send_sem=send.at[d], recv_sem=recv.at[d],
            device_id=(layers[d], seq), device_id_type=MESH,
        )

    first = []
    for d in range(1, n_seq):
        first.append(across(state_ref.at[peers[d]], parts.at[seq], send1, recv1, d))
        first.append(across(total_ref, factors.at[seq], send2, recv2, d))
    for copy in first:
        copy.start()
    asking = []
    for d in range(1, n_seq):
        asking.append(across(wanted_ref.at[peers[d]], asked_ref.at[seq], send3, recv3, d))
        asking[-1].start()
    parts[seq] = state_ref[seq]
    factors[seq] = total_ref[...]
    asked_ref[seq] = wanted_ref[seq]
    for copy in first:
        copy.wait()

    lanes = pl.ds(pl.multiple_of(lax.rem(seq, INNER // width) * width, width), width)

    def row_of(tile):
        for i in range(8):
            factor_row[:, i * 128 : (i + 1) * 128] = tile[i : i + 1, :]
        return factor_row[:, lanes]

    running = jnp.zeros((ROWS, width), F32)
    product = jnp.ones((8, 128), F32)
    for k in range(n_seq):
        sums[k] = running
        group_factor[k] = product
        running = row_of(factors[k]) * running + parts[k].astype(F32)
        product = product * factors[k]
    group_sum[grp] = running.astype(BF16)
    my_factor[grp] = product
    second = []
    for d in range(1, n_grp):
        second.append(along(group_sum.at[grp], group_sum.at[grp], send4, recv4, d))
        second.append(along(my_factor.at[grp], my_factor.at[grp], send5, recv5, d))
    for copy in second:
        copy.start()
    for copy in second:
        copy.wait()
    carry = jnp.zeros((ROWS, width), F32)
    for g in range(n_grp):
        new = row_of(my_factor[g]) * carry + group_sum[g].astype(F32)
        carry = jnp.where(g < grp, new, carry)
    for k in range(n_seq):
        shares[k] = (sums[k] + row_of(group_factor[k]) * carry).astype(BF16)
    third = []
    for d in range(1, n_seq):
        third.append(across(shares.at[peers[d]], before_ref.at[seq], send6, recv6, d))
        third[-1].start()
    before_ref[seq] = shares[seq]
    for copy in third:
        copy.wait()
    for copy in asking:
        copy.wait()


def prefix_part(state, total, wanted, n_grp, n_seq):
    spots = n_seq // 8
    width = INNER // spots
    sliced = state.reshape(8, ROWS, spots, width).swapaxes(1, 2).reshape(n_seq, ROWS, width)
    vmem = pl.BlockSpec(memory_space=pltpu.VMEM)
    dma = pltpu.SemaphoreType.DMA
    before, asked = pl.pallas_call(
        functools.partial(prefix_kernel, n_grp, n_seq),
        in_specs=[vmem] * 3,
        out_specs=[vmem] * 2,
        out_shape=[
            jax.ShapeDtypeStruct((n_seq, ROWS, width), BF16),
            jax.ShapeDtypeStruct(wanted.shape, jnp.int32),
        ],
        scratch_shapes=[
            pltpu.VMEM((n_seq, ROWS, width), BF16),
            pltpu.VMEM((n_seq, 8, 128), F32),
            pltpu.VMEM((n_seq, ROWS, width), F32),
            pltpu.VMEM((n_seq, 8, 128), F32),
            pltpu.VMEM((n_seq, ROWS, width), BF16),
            pltpu.VMEM((n_grp, ROWS, width), BF16),
            pltpu.VMEM((n_grp, 8, 128), F32),
            pltpu.VMEM((1, INNER), F32),
        ]
        + [dma((n_seq,))] * 6
        + [dma((n_grp,))] * 4
        + [dma((n_seq,))] * 2,
        compiler_params=pltpu.CompilerParams(
            collective_id=0, has_side_effects=True, vmem_limit_bytes=VMEM_LIMIT
        ),
        name="prefix_part",
    )(sliced, total, wanted)
    before = before.reshape(8, spots, ROWS, width).swapaxes(1, 2).reshape(NS, INNER)
    return before, asked


def finish_kernel(
    tokens_ref, xz_ref, maps_ref, intra_ref, reach_ref, state_ref, factor_ref, before_ref,
    skip_ref, gain2_ref, w_out_ref, gain3_ref, mid_ref, normed_ref, scaled,
):
    chunks = tokens_ref.shape[0] // CH
    spread = head_spread()
    group = lax.broadcasted_iota(jnp.int32, (256, 256), 0) // P_SIZE
    other = lax.broadcasted_iota(jnp.int32, (256, 256), 1) // P_SIZE
    same = (group == other).astype(BF16)
    for c in range(chunks):
        rows = slice(c * CH, (c + 1) * CH)
        state = state_ref[c] + factor_ref[c, 0:1] * before_ref[...].astype(F32)
        high = state.astype(BF16)
        low = (state - high.astype(F32)).astype(BF16)
        cmap = maps_ref[rows, NS:]
        reached = dot(
            jnp.concatenate([cmap, cmap], axis=1), jnp.concatenate([high, low], axis=0)
        )
        reach = dot_tn(split3(reach_ref[:, rows]), spread)
        mixed = intra_ref[rows] + reach * reached
        x = xz_ref[rows, :INNER].astype(F32)
        gate = xz_ref[rows, INNER:].astype(F32)
        gated = (mixed + skip_ref[...] * x) * (gate * jax.nn.sigmoid(gate))
        squares = (gated * gated).astype(BF16)
        power = jnp.concatenate(
            [dot(squares[:, i * 256 : (i + 1) * 256], same) for i in range(INNER // 256)], axis=1
        )
        scaled[rows] = (
            gated * lax.rsqrt(power * (1.0 / P_SIZE) + EPS) * gain2_ref[...]
        ).astype(BF16)
    middle = (tokens_ref[...].astype(F32) + dot(scaled[...], w_out_ref[...])).astype(BF16)
    mid_ref[...] = middle
    normed_ref[...] = rms_rows(middle, gain3_ref[...])


def finish_part(tokens, xz, maps, intra, reach, state, factor, before, skip, gain2, w_out, gain3):
    count = tokens.shape[0]
    tile = 2 * CH
    whole = lambda *shape: pl.BlockSpec(shape, lambda i: (0,) * len(shape))
    return pl.pallas_call(
        finish_kernel,
        grid=(count // tile,),
        in_specs=[
            pl.BlockSpec((tile, 512), lambda i: (i, 0)),
            pl.BlockSpec((tile, 2 * INNER), lambda i: (i, 0)),
            pl.BlockSpec((tile, 2 * NS), lambda i: (i, 0)),
            pl.BlockSpec((tile, INNER), lambda i: (i, 0)),
            pl.BlockSpec((H, tile), lambda i: (0, i)),
            pl.BlockSpec((2, NS, INNER), lambda i: (i, 0, 0)),
            pl.BlockSpec((2, 8, INNER), lambda i: (i, 0, 0)),
            whole(NS, INNER),
            whole(1, INNER),
            whole(1, INNER),
            whole(INNER, 512),
            whole(1, 512),
        ],
        out_specs=[pl.BlockSpec((tile, 512), lambda i: (i, 0))] * 2,
        out_shape=[jax.ShapeDtypeStruct((count, 512), BF16)] * 2,
        scratch_shapes=[pltpu.VMEM((tile, INNER), BF16)],
        compiler_params=pltpu.CompilerParams(vmem_limit_bytes=VMEM_LIMIT),
        name="finish_part",
    )(tokens, xz, maps, intra, reach, state, factor, before, skip, gain2, w_out, gain3)


def swap_kernel(n_seq, slots, asked_ref, normed_ref, arrived_ref, staged, send, recv, local):
    grp, seq = lax.axis_index("grp"), lax.axis_index("seq")
    barrier = pltpu.get_barrier_semaphore()
    for d in range(1, n_seq):
        pl.semaphore_signal(
            barrier, inc=1, device_id=(grp, lax.rem(seq + d, n_seq)), device_id_type=MESH
        )
    pl.semaphore_wait(barrier, n_seq - 1)
    copies = []
    for d in range(1, n_seq):
        peer = lax.rem(seq + d, n_seq)
        for j in range(slots):
            staged[d, j] = normed_ref[asked_ref[peer, j]]
        copies.append(
            pltpu.make_async_remote_copy(
                src_ref=staged.at[d], dst_ref=arrived_ref.at[seq],
                send_sem=send.at[d], recv_sem=recv.at[d],
                device_id=(grp, peer), device_id_type=MESH,
            )
        )
        copies[-1].start()
    for j in range(slots):
        staged[0, j] = normed_ref[asked_ref[seq, j]]
    own = pltpu.make_async_copy(staged.at[0], arrived_ref.at[seq], local)
    own.start()
    for copy in copies:
        copy.wait()
    own.wait()


def swap_part(asked, normed, n_seq):
    slots = asked.shape[1]
    vmem = pl.BlockSpec(memory_space=pltpu.VMEM)
    shape = (n_seq, slots, BL, 512)
    return pl.pallas_call(
        functools.partial(swap_kernel, n_seq, slots),
        in_specs=[pl.BlockSpec(memory_space=pltpu.SMEM), vmem],
        out_specs=pl.BlockSpec(memory_space=pl.ANY),
        out_shape=jax.ShapeDtypeStruct(shape, BF16),
        scratch_shapes=[
            pltpu.VMEM(shape, BF16),
            pltpu.SemaphoreType.DMA((n_seq,)),
            pltpu.SemaphoreType.DMA((n_seq,)),
            pltpu.SemaphoreType.DMA,
        ],
        compiler_params=pltpu.CompilerParams(
            collective_id=1, has_side_effects=True, vmem_limit_bytes=VMEM_LIMIT
        ),
        name="swap_part",
    )(asked, normed)


GROUP = 4
SPAN = (KN + 1) * BL


def attend_kernel(
    place_ref, normed_ref, mid_ref, arrived_ref, w_q_ref, w_kv_ref, w_o_ref, out_ref,
    sources, keys_values, queries, attended,
):
    step = pl.program_id(0)
    for i in range(GROUP):
        sources[i * SPAN : i * SPAN + BL] = normed_ref[i * BL : (i + 1) * BL]
        for k in range(KN):
            start = i * SPAN + (k + 1) * BL
            spot = place_ref[(step * GROUP + i) * KN + k]
            sources[start : start + BL] = arrived_ref[spot]
    keys_values[...] = dot(sources[...], w_kv_ref[...]).astype(BF16)
    queries[...] = (
        dot(normed_ref[...], w_q_ref[...]).astype(BF16).astype(F32) * (1.0 / math.sqrt(P_SIZE))
    ).astype(BF16)
    first_half = lax.broadcasted_iota(jnp.int32, (BL, 128), 1) < P_SIZE

    for i in range(GROUP):
        for p in range(PAIRS):
            lanes = slice(p * 128, (p + 1) * 128)
            values = slice(INNER + p * 128, INNER + (p + 1) * 128)
            q = queries[i * BL : (i + 1) * BL, lanes]
            zero = jnp.zeros_like(q)
            q = jnp.concatenate(
                [jnp.where(first_half, q, zero), jnp.where(first_half, zero, q)], axis=0
            )
            score = dot_nt(q, keys_values[i * SPAN : (i + 1) * SPAN, lanes])
            raised = jnp.exp(score - jnp.max(score, axis=-1, keepdims=True))
            weight = raised * (1.0 / jnp.sum(raised, axis=-1, keepdims=True))
            mixed = dot(weight.astype(BF16), keys_values[i * SPAN : (i + 1) * SPAN, values])
            attended[i * BL : (i + 1) * BL, lanes] = jnp.where(
                first_half, mixed[:BL], mixed[BL:]
            ).astype(BF16)
    out_ref[...] = (mid_ref[...].astype(F32) + dot(attended[...], w_o_ref[...])).astype(BF16)


def attend_part(place, normed, mid, arrived, w_q, w_kv, w_o):
    count = normed.shape[0]
    tile = GROUP * BL
    whole = lambda *shape: pl.BlockSpec(shape, lambda i, place: (0,) * len(shape))
    return pl.pallas_call(
        attend_kernel,
        grid_spec=pltpu.PrefetchScalarGridSpec(
            num_scalar_prefetch=1,
            grid=(count // tile,),
            in_specs=[
                pl.BlockSpec((tile, 512), lambda i, place: (i, 0)),
                pl.BlockSpec((tile, 512), lambda i, place: (i, 0)),
                whole(*arrived.shape),
                whole(512, INNER),
                whole(512, 2 * INNER),
                whole(INNER, 512),
            ],
            out_specs=pl.BlockSpec((tile, 512), lambda i, place: (i, 0)),
            scratch_shapes=[
                pltpu.VMEM((GROUP * SPAN, 512), BF16),
                pltpu.VMEM((GROUP * SPAN, 2 * INNER), BF16),
                pltpu.VMEM((tile, INNER), BF16),
                pltpu.VMEM((tile, INNER), BF16),
            ],
        ),
        out_shape=jax.ShapeDtypeStruct((count, 512), BF16),
        compiler_params=pltpu.CompilerParams(vmem_limit_bytes=VMEM_LIMIT),
        name="attend_part",
    )(place, normed, mid, arrived, w_q, w_kv, w_o)


def per_device(
    n_grp, n_seq, tokens, norm_gain1, w_xz, w_bc, w_dt, dt_bias, decay_rate, curve_jump,
    skip_gain, norm_gain2, w_out, norm_gain3, w_q, w_kv, w_o, nbr_owner, nbr_block,
):
    count = tokens.shape[0]
    blocks = count // BL
    requests = blocks * KN
    slots = max(2, -(-requests // n_seq))
    owner = nbr_owner.reshape(-1)
    block = nbr_block.reshape(-1)
    order = jnp.arange(requests)
    earlier = (owner[:, None] == owner[None, :]) & (order[None, :] < order[:, None])
    rank = jnp.sum(earlier.astype(jnp.int32), axis=1)
    place = owner * slots + rank
    hit = place[None, :] == jnp.arange(n_seq * slots, dtype=jnp.int32)[:, None]
    wanted = jnp.sum(jnp.where(hit, block[None, :], 0), axis=1).reshape(n_seq, 1, slots)
    wanted = jnp.pad(wanted, ((0, 0), (0, 7), (0, 128 - slots)))

    xz, maps, intra, reach, state, factor, total, final = local_part(
        tokens, norm_gain1[None], w_xz, w_bc, w_dt, dt_bias[:, None], decay_rate[:, None],
        curve_jump.reshape(count // CH, 1, CH),
    )
    before, asked = prefix_part(final, total, wanted, n_grp, n_seq)
    mid, normed = finish_part(
        tokens, xz, maps, intra, reach, state, factor, before,
        jnp.repeat(skip_gain, P_SIZE)[None], norm_gain2[None], w_out, norm_gain3[None],
    )
    arrived = swap_part(asked[:, 0, :slots], normed.reshape(blocks, BL, 512), n_seq)
    return attend_part(
        place, normed, mid, arrived.reshape(n_seq * slots, BL, 512), w_q, w_kv, w_o
    )


def solution(mesh):
    shard = P(("grp", "seq"), None)
    in_specs = (
        shard, P(), P(), P(), P(), P(), P(), P(("grp", "seq")), P(), P(), P(), P(), P(), P(),
        P(), shard, shard,
    )
    body = functools.partial(per_device, mesh.shape["grp"], mesh.shape["seq"])
    return jax.shard_map(body, mesh=mesh, in_specs=in_specs, out_specs=shard, check_vma=False)
```

profile of v0, /device:TPU:1, one launch (start us, length us, event | category | flops | bytes accessed | tf_op | source)
XLA Modules:
  0.0 140.4 jit_solution(3823983171869940582)
XLA Ops:
  0.0 1.3 copy.36.bias_ref
  1.3 1.3 copy.37.rate_ref
  2.6 0.7 broadcast_in_dim.42
  3.4 0.7 broadcast_in_dim_reshape.2.skip_ref
  4.0 0.8 copy.34
  4.8 0.1 reshape.26
  4.9 0.2 convert_reduce_fusion
  5.1 0.0 copy-start
  5.1 0.8 copy.38
  5.8 0.1 broadcast_in_dim.39
  5.9 0.1 select_reduce_fusion
  6.0 0.1 reshape.28
  6.1 0.6 pad.4.wanted_ref
  6.7 1.5 %copy.35.w_dt_ref = bf16[512,16]{1,0:T(8,128)(2,1)} copy(bf16[512,16]{0,1:T(8,128)(2,1)} %param.21) | data formatting | bytes 32768 | tf_op args[4]
  8.2 15.0 %local_part.1 = (bf16[1024,2048]{1,0:T(8,128)(2,1)}, bf16[1024,256]{1,0:T(8,128)(2,1)}, f32[1024,1024]{1,0:T(8,128)}, f32[16,1024]{1,0:T(8,128)}, f32[8,128,1024...) custom-call(bf16[1024,512]{1,0:T(8,128)(2,1)} %tokens_ref.3, ...), custom_call_target="tpu_custom_call" | custom-call | tf_op jit(solution)/shard_map/local_part/pallas_call | solution.py:132
  23.2 21.2 %prefix_part.1 = (bf16[8,16,1024]{2,1,0:T(8,128)(2,1)}, s32[8,8,128]{2,1,0:T(8,128)}) custom-call(bf16[8,16,1024]{2,1,0:T(8,128)(2,1)} %bitcast.15, f32[8,128]{1,0:T(8,128)} %get-tuple-element.24.total_ref, s32[8,8,128]{2,1,0:T(8,128)} %pad.4.wanted_ref), custom_call_target="tpu_custom_call" | custom-call | tf_op jit(solution)/shard_map/prefix_part/pallas_call | solution.py:271
  44.4 10.8 %finish_part.1 = (bf16[1024,512]{1,0:T(8,128)(2,1)}, bf16[1024,512]{1,0:T(8,128)(2,1)}) custom-call(bf16[1024,512]{1,0:T(8,128)(2,1)} %tokens_ref.3, bf16[1024,2048]{1,0:T(8,128)(2,1)} %get-tuple-element.17.xz_ref, bf16[1024,256]{1,0:T(8,128)(2,1)} %get-tuple-element.18.maps_ref, f32[1024,1024]{1,0:T(8,128)} %get-tuple-element.19.intra_ref, ...), custom_call_target="tpu_custom_call" | custom-call | tf_op jit(solution)/shard_map/finish_part/pallas_call | solution.py:340
  55.2 0.0 copy-done
  55.2 1.4 slice.3
  56.5 27.6 %swap_part.1 = bf16[8,4,64,512]{3,2,1,0:T(8,128)(2,1)} custom-call(s32[8,4]{1,0:T(8,128)} %bitcast.16, bf16[16,64,512]{2,1,0:T(8,128)(2,1)} %bitcast.13), custom_call_target="tpu_custom_call" | custom-call | tf_op jit(solution)/shard_map/swap_part/pallas_call | solution.py:399
  84.2 56.2 %attend_part.1 = bf16[1024,512]{1,0:T(8,128)(2,1)} custom-call(s32[32]{0:T(128)} %copy-done, bf16[1024,512]{1,0:T(8,128)(2,1)} %get-tuple-element.26.normed_ref, bf16[1024,512]{1,0:T(8,128)(2,1)} %get-tuple-element.27.mid_ref, bf16[32,64,512]{2,1,0:T(8,128)(2,1)} %bitcast.12, bf16[512,1024]{1,0:T(8,128)(2,1)} %w_q_ref.1, bf16[512,2048]{1,0:T(8,128)(2,1)} %w_kv_ref.1, ...), custom_call_target="tpu_custom_call" | custom-call | tf_op jit(solution)/shard_map/attend_part/pallas_call | solution.py:461
  (1 shorter events, 0.0 us)
Async XLA Ops:
  5.1 50.1 %copy-start = (s32[32]{0:T(128)}, s32[32]{0:T(128)S(1)}, u32[]{:S(2)}) copy-start(s32[32]{0:T(128)S(1)} %multiply_add_fusion.place_ref) | copy-start | bytes 388
where the time goes:
time: 141 us; the launch traced here: 140 us
  Pallas kernels  131 us (93%)
  local copies, waits for them, and re-layouts  9.24 us (7%)
    pallas_call x1, Pallas kernels, attend_part(): pl.pallas_call(attend_kernel, grid_spec=pltpu.PrefetchScalarGridSpec(num_...  56.2 us
    pallas_call x1, Pallas kernels, swap_part(): pl.pallas_call(functools.partial(swap_kernel, n_seq, slots), in_specs=[pl...  27.6 us
    pallas_call x1, Pallas kernels, prefix_part(): pl.pallas_call(functools.partial(prefix_kernel, n_grp, n_seq), in_specs=[...  21.2 us
    pallas_call x1, Pallas kernels, local_part(): pl.pallas_call(local_kernel, grid=(count // tile,), in_specs=[pl.BlockSpe...  15 us
    pallas_call x1, Pallas kernels, finish_part(): pl.pallas_call(finish_kernel, grid=(count // tile,), in_specs=[pl.BlockSp...  10.8 us
    unnamed x5, local copies, waits for them, and re-layouts  2.98 us

commit v1 on v0

--- a/solution.py
+++ b/solution.py
@@ -56,6 +56,12 @@
     return (head == lane).astype(BF16)
 
 
+def column(row):
+    down = lax.broadcasted_iota(jnp.int32, (H, H), 0)
+    along = lax.broadcasted_iota(jnp.int32, (H, H), 1)
+    return jnp.sum(jnp.where(down == along, row, 0.0), axis=1, keepdims=True)
+
+
 def local_kernel(
     tokens_ref, gain_ref, w_xz_ref, w_bc_ref, w_dt_ref, bias_ref, rate_ref, jump_ref,
     xz_ref, maps_ref, intra_ref, reach_ref, state_ref, factor_ref, total_ref, final_ref,
@@ -73,11 +79,9 @@
     xz_ref[...] = dot(normed, w_xz_ref[...]).astype(BF16)
     maps_ref[...] = dot(normed, w_bc_ref[...]).astype(BF16)
     steps_t = jax.nn.softplus(
-        lax.dot_general(
-            w_dt_ref[...], normed, (((0,), (1,)), ((), ())), preferred_element_type=F32
-        )
-        + bias_ref[...]
+        dot_nt(w_dt_ref[...], normed) + column(bias_ref[...])
     )
+    rate = column(rate_ref[...])
     row = lax.broadcasted_iota(jnp.int32, (CH, CH), 0)
     col = lax.broadcasted_iota(jnp.int32, (CH, CH), 1)
     lower = row >= col
@@ -87,7 +91,7 @@
     for c in range(chunks):
         rows = slice(c * CH, (c + 1) * CH)
         u_t = steps_t[:, rows]
-        decay_t = -(rate_ref[...] * u_t + jump_ref[c])
+        decay_t = -(rate * u_t + jump_ref[c])
         run_t = jnp.dot(decay_t, upto, precision=lax.Precision.HIGHEST, preferred_element_type=F32)
         run = jnp.concatenate([run_t, jnp.zeros((CH - H, CH), F32)], axis=0).T
         reach_t = jnp.exp(run_t)
@@ -137,9 +141,9 @@
             whole(1, 512),
             whole(512, 2 * INNER),
             whole(512, 2 * NS),
-            whole(512, H),
-            whole(H, 1),
-            whole(H, 1),
+            whole(H, 512),
+            whole(1, H),
+            whole(1, H),
             pl.BlockSpec((2, 1, CH), lambda i: (i, 0, 0)),
         ],
         out_specs=[
@@ -307,6 +311,7 @@
     group = lax.broadcasted_iota(jnp.int32, (256, 256), 0) // P_SIZE
     other = lax.broadcasted_iota(jnp.int32, (256, 256), 1) // P_SIZE
     same = (group == other).astype(BF16)
+    skip = dot_tn(split3(jnp.broadcast_to(column(skip_ref[...]), (H, 8))), spread)[0:1]
     for c in range(chunks):
         rows = slice(c * CH, (c + 1) * CH)
         state = state_ref[c] + factor_ref[c, 0:1] * before_ref[...].astype(F32)
@@ -320,7 +325,7 @@
         mixed = intra_ref[rows] + reach * reached
         x = xz_ref[rows, :INNER].astype(F32)
         gate = xz_ref[rows, INNER:].astype(F32)
-        gated = (mixed + skip_ref[...] * x) * (gate * jax.nn.sigmoid(gate))
+        gated = (mixed + skip * x) * (gate * jax.nn.sigmoid(gate))
         squares = (gated * gated).astype(BF16)
         power = jnp.concatenate(
             [dot(squares[:, i * 256 : (i + 1) * 256], same) for i in range(INNER // 256)], axis=1
@@ -349,7 +354,7 @@
             pl.BlockSpec((2, NS, INNER), lambda i: (i, 0, 0)),
             pl.BlockSpec((2, 8, INNER), lambda i: (i, 0, 0)),
             whole(NS, INNER),
-            whole(1, INNER),
+            whole(1, H),
             whole(1, INNER),
             whole(INNER, 512),
             whole(1, 512),
@@ -362,8 +367,26 @@
     )(tokens, xz, maps, intra, reach, state, factor, before, skip, gain2, w_out, gain3)
 
 
-def swap_kernel(n_seq, slots, asked_ref, normed_ref, arrived_ref, staged, send, recv, local):
+SPAN = (KN + 1) * BL
+QUADS = INNER // 256
+PAIRED = 2
+
+
+def attend_kernel(
+    n_seq, slots, asked_ref, place_ref, normed_ref, mid_ref, w_q_hbm, w_kv_hbm, w_o_hbm, out_ref,
+    w_q_ref, w_kv_ref, w_o_ref, staged, arrived, keys_values, queries, scores, attended,
+    send, recv, loads,
+):
     grp, seq = lax.axis_index("grp"), lax.axis_index("seq")
+    blocks = normed_ref.shape[0]
+    fetches = [
+        pltpu.make_async_copy(src, dst, loads.at[i])
+        for i, (src, dst) in enumerate(
+            [(w_kv_hbm, w_kv_ref), (w_q_hbm, w_q_ref), (w_o_hbm, w_o_ref)]
+        )
+    ]
+    for fetch in fetches:
+        fetch.start()
     barrier = pltpu.get_barrier_semaphore()
     for d in range(1, n_seq):
         pl.semaphore_signal(
@@ -374,115 +397,134 @@
     for d in range(1, n_seq):
         peer = lax.rem(seq + d, n_seq)
         for j in range(slots):
-            staged[d, j] = normed_ref[asked_ref[peer, j]]
+            staged[d, j] = normed_ref[asked_ref[peer, 0, j]]
         copies.append(
             pltpu.make_async_remote_copy(
-                src_ref=staged.at[d], dst_ref=arrived_ref.at[seq],
+                src_ref=staged.at[d], dst_ref=arrived.at[seq],
                 send_sem=send.at[d], recv_sem=recv.at[d],
                 device_id=(grp, peer), device_id_type=MESH,
             )
         )
         copies[-1].start()
+    for fetch in fetches:
+        fetch.wait()
+    group = 4
+    quarter = lax.broadcasted_iota(jnp.int32, (BL, 256), 1) // P_SIZE
+
+    def own_blocks(t, carry):
+        rows = normed_ref[pl.ds(t * group, group)].reshape(group * BL, 512)
+        keys_values[pl.ds(t * group, group)] = (
+            dot(rows, w_kv_ref[...]).astype(BF16).reshape(group, BL, 2 * INNER)
+        )
+        asking = (
+            dot(rows, w_q_ref[...]).astype(BF16).astype(F32) * (1.0 / math.sqrt(P_SIZE))
+        ).astype(BF16)
+        for i in range(group):
+            for u in range(QUADS):
+                q = asking[i * BL : (i + 1) * BL, u * 256 : (u + 1) * 256]
+                zero = jnp.zeros_like(q)
+                queries[t * group + i, u] = jnp.concatenate(
+                    [jnp.where(quarter == h, q, zero) for h in range(4)], axis=0
+                )
+        return carry
+
+    lax.fori_loop(0, blocks // group, own_blocks, 0)
     for j in range(slots):
-        staged[0, j] = normed_ref[asked_ref[seq, j]]
-    own = pltpu.make_async_copy(staged.at[0], arrived_ref.at[seq], local)
-    own.start()
+        keys_values[blocks + seq * slots + j] = keys_values[asked_ref[seq, 0, j]]
+    for d in range(1, n_seq):
+        origin = lax.rem(seq + n_seq - d, n_seq)
+        copies[d - 1].wait_recv()
+        rows = arrived[origin].reshape(slots * BL, 512)
+        keys_values[pl.ds(blocks + origin * slots, slots)] = (
+            dot(rows, w_kv_ref[...]).astype(BF16).reshape(slots, BL, 2 * INNER)
+        )
+
+    first_half = lax.broadcasted_iota(jnp.int32, (BL, 128), 1) < P_SIZE
+
+    def attend(t, carry):
+        units = [(i, u) for i in range(PAIRED) for u in range(QUADS)]
+        spots = [
+            [t * PAIRED + i]
+            + [blocks + place_ref[k * blocks + t * PAIRED + i] for k in range(KN)]
+            for i in range(PAIRED)
+        ]
+
+        def score(n):
+            i, u = units[n]
+            keys = jnp.concatenate(
+                [keys_values[spot, :, u * 256 : (u + 1) * 256] for spot in spots[i]], axis=0
+            )
+            scores[n] = dot_nt(keys, queries[t * PAIRED + i, u])
+
+        def mix(n):
+            i, u = units[n]
+            for half in range(2):
+                lanes = slice(u * 256 + half * 128, u * 256 + (half + 1) * 128)
+                values = slice(INNER + lanes.start, INNER + lanes.stop)
+                part = scores[n, :, half * 128 : (half + 1) * 128]
+                raised = jnp.exp(part - jnp.max(part, axis=0, keepdims=True))
+                weight = raised * (1.0 / jnp.sum(raised, axis=0, keepdims=True))
+                value = jnp.concatenate(
+                    [keys_values[spot, :, values] for spot in spots[i]], axis=0
+                )
+                mixed = dot_tn(weight.astype(BF16), value)
+                attended[pl.ds((t * PAIRED + i) * BL, BL), lanes] = jnp.where(
+                    first_half, mixed[:BL], mixed[BL:]
+                ).astype(BF16)
+
+        ahead = 3
+        for n in range(len(units) + ahead):
+            if n < len(units):
+                score(n)
+            if n >= ahead:
+                mix(n - ahead)
+        return carry
+
+    lax.fori_loop(0, blocks // PAIRED, attend, 0)
+
+    def project(t, carry):
+        rows = pl.ds(t * 256, 256)
+        out_ref[rows] = (
+            mid_ref[rows].astype(F32) + dot(attended[rows], w_o_ref[...])
+        ).astype(BF16)
+        return carry
+
+    lax.fori_loop(0, blocks * BL // 256, project, 0)
     for copy in copies:
-        copy.wait()
-    own.wait()
-
-
-def swap_part(asked, normed, n_seq):
-    slots = asked.shape[1]
+        copy.wait_send()
+
+
+def attend_part(asked, place, normed, mid, w_q, w_kv, w_o, n_seq, slots):
+    count = mid.shape[0]
+    blocks = count // BL
     vmem = pl.BlockSpec(memory_space=pltpu.VMEM)
-    shape = (n_seq, slots, BL, 512)
+    smem = pl.BlockSpec(memory_space=pltpu.SMEM)
+    anywhere = pl.BlockSpec(memory_space=pl.ANY)
+    dma = pltpu.SemaphoreType.DMA
     return pl.pallas_call(
-        functools.partial(swap_kernel, n_seq, slots),
-        in_specs=[pl.BlockSpec(memory_space=pltpu.SMEM), vmem],
-        out_specs=pl.BlockSpec(memory_space=pl.ANY),
-        out_shape=jax.ShapeDtypeStruct(shape, BF16),
+        functools.partial(attend_kernel, n_seq, slots),
+        in_specs=[smem, smem, vmem, vmem, anywhere, anywhere, anywhere],
+        out_specs=vmem,
+        out_shape=jax.ShapeDtypeStruct((count, 512), BF16),
         scratch_shapes=[
-            pltpu.VMEM(shape, BF16),
-            pltpu.SemaphoreType.DMA((n_seq,)),
-            pltpu.SemaphoreType.DMA((n_seq,)),
-            pltpu.SemaphoreType.DMA,
+            pltpu.VMEM(w_q.shape, BF16),
+            pltpu.VMEM(w_kv.shape, BF16),
+            pltpu.VMEM(w_o.shape, BF16),
+            pltpu.VMEM((n_seq, slots, BL, 512), BF16),
+            pltpu.VMEM((n_seq, slots, BL, 512), BF16),
+            pltpu.VMEM((blocks + n_seq * slots, BL, 2 * INNER), BF16),
+            pltpu.VMEM((blocks, QUADS, 256, 256), BF16),
+            pltpu.VMEM((PAIRED * QUADS, SPAN, 256), F32),
+            pltpu.VMEM((count, INNER), BF16),
+            dma((n_seq,)),
+            dma((n_seq,)),
+            dma((3,)),
         ],
         compiler_params=pltpu.CompilerParams(
             collective_id=1, has_side_effects=True, vmem_limit_bytes=VMEM_LIMIT
         ),
-        name="swap_part",
-    )(asked, normed)
-
-
-GROUP = 4
-SPAN = (KN + 1) * BL
-
-
-def attend_kernel(
-    place_ref, normed_ref, mid_ref, arrived_ref, w_q_ref, w_kv_ref, w_o_ref, out_ref,
-    sources, keys_values, queries, attended,
-):
-    step = pl.program_id(0)
-    for i in range(GROUP):
-        sources[i * SPAN : i * SPAN + BL] = normed_ref[i * BL : (i + 1) * BL]
-        for k in range(KN):
-            start = i * SPAN + (k + 1) * BL
-            spot = place_ref[(step * GROUP + i) * KN + k]
-            sources[start : start + BL] = arrived_ref[spot]
-    keys_values[...] = dot(sources[...], w_kv_ref[...]).astype(BF16)
-    queries[...] = (
-        dot(normed_ref[...], w_q_ref[...]).astype(BF16).astype(F32) * (1.0 / math.sqrt(P_SIZE))
-    ).astype(BF16)
-    first_half = lax.broadcasted_iota(jnp.int32, (BL, 128), 1) < P_SIZE
-
-    for i in range(GROUP):
-        for p in range(PAIRS):
-            lanes = slice(p * 128, (p + 1) * 128)
-            values = slice(INNER + p * 128, INNER + (p + 1) * 128)
-            q = queries[i * BL : (i + 1) * BL, lanes]
-            zero = jnp.zeros_like(q)
-            q = jnp.concatenate(
-                [jnp.where(first_half, q, zero), jnp.where(first_half, zero, q)], axis=0
-            )
-            score = dot_nt(q, keys_values[i * SPAN : (i + 1) * SPAN, lanes])
-            raised = jnp.exp(score - jnp.max(score, axis=-1, keepdims=True))
-            weight = raised * (1.0 / jnp.sum(raised, axis=-1, keepdims=True))
-            mixed = dot(weight.astype(BF16), keys_values[i * SPAN : (i + 1) * SPAN, values])
-            attended[i * BL : (i + 1) * BL, lanes] = jnp.where(
-                first_half, mixed[:BL], mixed[BL:]
-            ).astype(BF16)
-    out_ref[...] = (mid_ref[...].astype(F32) + dot(attended[...], w_o_ref[...])).astype(BF16)
-
-
-def attend_part(place, normed, mid, arrived, w_q, w_kv, w_o):
-    count = normed.shape[0]
-    tile = GROUP * BL
-    whole = lambda *shape: pl.BlockSpec(shape, lambda i, place: (0,) * len(shape))
-    return pl.pallas_call(
-        attend_kernel,
-        grid_spec=pltpu.PrefetchScalarGridSpec(
-            num_scalar_prefetch=1,
-            grid=(count // tile,),
-            in_specs=[
-                pl.BlockSpec((tile, 512), lambda i, place: (i, 0)),
-                pl.BlockSpec((tile, 512), lambda i, place: (i, 0)),
-                whole(*arrived.shape),
-                whole(512, INNER),
-                whole(512, 2 * INNER),
-                whole(INNER, 512),
-            ],
-            out_specs=pl.BlockSpec((tile, 512), lambda i, place: (i, 0)),
-            scratch_shapes=[
-                pltpu.VMEM((GROUP * SPAN, 512), BF16),
-                pltpu.VMEM((GROUP * SPAN, 2 * INNER), BF16),
-                pltpu.VMEM((tile, INNER), BF16),
-                pltpu.VMEM((tile, INNER), BF16),
-            ],
-        ),
-        out_shape=jax.ShapeDtypeStruct((count, 512), BF16),
-        compiler_params=pltpu.CompilerParams(vmem_limit_bytes=VMEM_LIMIT),
         name="attend_part",
-    )(place, normed, mid, arrived, w_q, w_kv, w_o)
+    )(asked, place, normed, mid, w_q, w_kv, w_o)
 
 
 def per_device(
@@ -493,8 +535,8 @@
     blocks = count // BL
     requests = blocks * KN
     slots = max(2, -(-requests // n_seq))
-    owner = nbr_owner.reshape(-1)
-    block = nbr_block.reshape(-1)
+    owner = nbr_owner.T.reshape(-1)
+    block = nbr_block.T.reshape(-1)
     order = jnp.arange(requests)
     earlier = (owner[:, None] == owner[None, :]) & (order[None, :] < order[:, None])
     rank = jnp.sum(earlier.astype(jnp.int32), axis=1)
@@ -504,17 +546,16 @@
     wanted = jnp.pad(wanted, ((0, 0), (0, 7), (0, 128 - slots)))
 
     xz, maps, intra, reach, state, factor, total, final = local_part(
-        tokens, norm_gain1[None], w_xz, w_bc, w_dt, dt_bias[:, None], decay_rate[:, None],
+        tokens, norm_gain1[None], w_xz, w_bc, w_dt.T, dt_bias[None], decay_rate[None],
         curve_jump.reshape(count // CH, 1, CH),
     )
     before, asked = prefix_part(final, total, wanted, n_grp, n_seq)
     mid, normed = finish_part(
         tokens, xz, maps, intra, reach, state, factor, before,
-        jnp.repeat(skip_gain, P_SIZE)[None], norm_gain2[None], w_out, norm_gain3[None],
+        skip_gain[None], norm_gain2[None], w_out, norm_gain3[None],
     )
-    arrived = swap_part(asked[:, 0, :slots], normed.reshape(blocks, BL, 512), n_seq)
     return attend_part(
-        place, normed, mid, arrived.reshape(n_seq * slots, BL, 512), w_q, w_kv, w_o
+        asked, place, normed.reshape(blocks, BL, 512), mid, w_q, w_kv, w_o, n_seq, slots
     )
 
 

time: 141 us -> 94.9 us (0.67)
  Pallas kernels: 131 us -> 89.8 us
  local copies, waits for them, and re-layouts: 9.24 us -> 4.48 us
    pallas_call x2 -> x1, Pallas kernels: 83.8 us -> 42.5 us  [attend_part(): pl.pallas_call(functools.partial(attend_kernel, n_seq, slots), in_specs=[...]
    broadcast_in_dim x3 -> x0, local copies, waits for them, and re-layouts: 3.37 us -> none  [the longest x1 1.33 us: per_device(): decay_rate[:, None]]
    unnamed x5 -> x3, local copies, waits for them, and re-layouts: 2.98 us -> 2.27 us
where the time goes in v1:
time: 94.9 us; the launch traced here: 94.6 us
  Pallas kernels  89.8 us (95%)
  local copies, waits for them, and re-layouts  4.48 us (5%)
    pallas_call x1, Pallas kernels, attend_part(): pl.pallas_call(functools.partial(attend_kernel, n_seq, slots), in_specs=[...  42.5 us
    pallas_call x1, Pallas kernels, prefix_part(): pl.pallas_call(functools.partial(prefix_kernel, n_grp, n_seq), in_specs=[...  21.2 us
    pallas_call x1, Pallas kernels, local_part(): pl.pallas_call(local_kernel, grid=(count // tile,), in_specs=[pl.BlockSpe...  15 us
    pallas_call x1, Pallas kernels, finish_part(): pl.pallas_call(finish_kernel, grid=(count // tile,), in_specs=[pl.BlockSp...  11.1 us
    unnamed x3, local copies, waits for them, and re-layouts  2.27 us

profile of v1, /device:TPU:1, one launch (start us, length us, event | category | flops | bytes accessed | tf_op | source)
XLA Modules:
  0.0 94.6 jit_solution(5179340577890642468)
XLA Ops:
  0.0 0.8 reshape.24
  0.8 0.2 convert_reduce_fusion
  0.9 0.0 copy-start
  1.0 0.8 broadcast_in_dim.39
  1.7 0.1 select_reduce_fusion
  1.8 0.1 reshape.25
  1.9 0.6 pad.4.wanted_ref
  2.5 15.0 %local_part.1 = (bf16[1024,2048]{1,0:T(8,128)(2,1)}, bf16[1024,256]{1,0:T(8,128)(2,1)}, f32[1024,1024]{1,0:T(8,128)}, f32[16,1024]{1,0:T(8,128)}, f32[8,128,1024...) custom-call(bf16[1024,512]{1,0:T(8,128)(2,1)} %tokens_ref.3, ...), custom_call_target="tpu_custom_call" | custom-call | tf_op jit(solution)/shard_map/local_part/pallas_call | solution.py:136
  17.6 21.2 %prefix_part.1 = (bf16[8,16,1024]{2,1,0:T(8,128)(2,1)}, s32[8,8,128]{2,1,0:T(8,128)}) custom-call(bf16[8,16,1024]{2,1,0:T(8,128)(2,1)} %bitcast.16, f32[8,128]{1,0:T(8,128)} %get-tuple-element.18.total_ref, s32[8,8,128]{2,1,0:T(8,128)} %pad.4.wanted_ref), custom_call_target="tpu_custom_call" | custom-call | tf_op jit(solution)/shard_map/prefix_part/pallas_call | solution.py:275
  38.7 11.1 %finish_part.1 = (bf16[1024,512]{1,0:T(8,128)(2,1)}, bf16[1024,512]{1,0:T(8,128)(2,1)}) custom-call(bf16[1024,512]{1,0:T(8,128)(2,1)} %tokens_ref.3, bf16[1024,2048]{1,0:T(8,128)(2,1)} %get-tuple-element.20.xz_ref, bf16[1024,256]{1,0:T(8,128)(2,1)} %get-tuple-element.21.maps_ref, f32[1024,1024]{1,0:T(8,128)} %get-tuple-element.22.intra_ref, ...), custom_call_target="tpu_custom_call" | custom-call | tf_op jit(solution)/shard_map/finish_part/pallas_call | solution.py:345
  49.8 0.0 copy-done
  49.8 42.5 %attend_part.1 = bf16[1024,512]{1,0:T(8,128)(2,1)} custom-call(s32[8,8,128]{2,1,0:T(8,128)} %get-tuple-element.19.asked_ref, s32[32]{0:T(128)} %copy-done, bf16[16,64,512]{2,1,0:T(8,128)(2,1)} %bitcast.14, bf16[1024,512]{1,0:T(8,128)(2,1)} %get-tuple-element.28.mid_ref, bf16[512,1024]{1,0:T(8,128)(2,1)} %w_q_hbm.1, bf16[512,2048]{1,0:T(8,128)(2,1)} %w_kv_hbm.1, ...), custom_call_target="tpu_custom_call" | custom-call | tf_op jit(solution)/shard_map/attend_part/pallas_call | solution.py:504
  92.3 2.3 %copy.22 = bf16[1024,512]{1,0:T(8,128)(2,1)} copy(bf16[1024,512]{1,0:T(8,128)(2,1)} %attend_part.1) | data formatting | bytes 2097152
  (1 shorter events, 0.0 us)
Async XLA Ops:
  0.9 48.9 %copy-start = (s32[32]{0:T(128)}, s32[32]{0:T(128)S(1)}, u32[]{:S(2)}) copy-start(s32[32]{0:T(128)S(1)} %multiply_add_fusion.place_ref) | copy-start | bytes 388

commit v2 on v1

v2 whole, which is shorter than its diff:
```python
import functools
import math

import jax
import jax.numpy as jnp
from jax import lax
from jax.experimental import pallas as pl
from jax.experimental.pallas import tpu as pltpu
from jax.sharding import PartitionSpec as P

H = 16
P_SIZE = 64
NS = 128
INNER = 1024
CH = 128
BL = 64
KN = 2
PAIRS = INNER // 128
ROWS = 16
SPAN = (KN + 1) * BL
QUADS = INNER // 256
PAIRED = 2
EPS = 1e-05
VMEM_LIMIT = 60 * 1024 * 1024
MESH = pl.DeviceIdType.MESH
F32 = jnp.float32
BF16 = jnp.bfloat16


def dot(a, b):
    return jnp.dot(a, b, preferred_element_type=F32)


def dot_nt(a, b):
    return lax.dot_general(a, b, (((1,), (1,)), ((), ())), preferred_element_type=F32)


def dot_tn(a, b):
    return lax.dot_general(a, b, (((0,), (0,)), ((), ())), preferred_element_type=F32)


def rms_rows(values, weights):
    floats = values.astype(F32)
    scale = lax.rsqrt(jnp.mean(floats * floats, axis=-1, keepdims=True) + EPS)
    return (floats * scale * weights).astype(BF16)


def split3(values):
    high = values.astype(BF16)
    rest = values - high.astype(F32)
    middle = rest.astype(BF16)
    low = (rest - middle.astype(F32)).astype(BF16)
    return jnp.concatenate([high, middle, low], axis=0)


def head_spread():
    head = lax.broadcasted_iota(jnp.int32, (3 * H, INNER), 0) % H
    lane = lax.broadcasted_iota(jnp.int32, (3 * H, INNER), 1) // P_SIZE
    return (head == lane).astype(BF16)


def column(row):
    down = lax.broadcasted_iota(jnp.int32, (H, H), 0)
    along = lax.broadcasted_iota(jnp.int32, (H, H), 1)
    return jnp.sum(jnp.where(down == along, row, 0.0), axis=1, keepdims=True)


def int_column(row):
    size = row.shape[1]
    down = lax.broadcasted_iota(jnp.int32, (size, size), 0)
    along = lax.broadcasted_iota(jnp.int32, (size, size), 1)
    return jnp.sum(jnp.where(down == along, row, 0), axis=1, keepdims=True)


def request_lists(n_seq, slots, owner_ref, block_ref, wanted, place):
    blocks = owner_ref.shape[1]
    down = lax.broadcasted_iota(jnp.int32, (blocks, blocks), 0)
    along = lax.broadcasted_iota(jnp.int32, (blocks, blocks), 1)
    rows = [owner_ref[k : k + 1, :] for k in range(KN)]
    columns = [int_column(row) for row in rows]
    places = []
    for k in range(KN):
        rank = jnp.sum(
            jnp.where((columns[k] == rows[k]) & (down < along), 1, 0), axis=0, keepdims=True
        )
        for j in range(k):
            rank = rank + jnp.sum(
                jnp.where(columns[j] == rows[k], 1, 0), axis=0, keepdims=True
            )
        places.append(rows[k] * slots + rank)
        place[k : k + 1, :blocks] = places[k]
    slot = lax.broadcasted_iota(jnp.int32, (8, blocks), 0)
    for p in range(n_seq):
        named = jnp.zeros((8, 1), jnp.int32)
        for k in range(KN):
            hit = (places[k] == slot + p * slots) & (slot < slots)
            named = named + jnp.sum(
                jnp.where(hit, block_ref[k : k + 1, :], 0), axis=1, keepdims=True
            )
        wanted[p] = jnp.broadcast_to(named, (8, 128))


def layer_kernel(
    n_grp, n_seq, slots,
    tokens_ref, gain_ref, w_bc_ref, w_dt_ref, bias_ref, rate_ref, jump_ref, skip_ref,
    gain2_ref, gain3_ref, owner_ref, block_ref,
    w_xz_hbm, w_out_hbm, w_q_hbm, w_kv_hbm, w_o_hbm,
    out_ref,
    w_xz_ref, w_out_ref, w_q_ref, w_kv_ref, w_o_ref,
    xz_ref, maps_ref, pre_ref, state_ref, step_ref, run_ref, base_ref, carried,
    mid_ref, normed_ref, queries, scores,
    final, total, wanted, asked, asked_here, place, place_here,
    parts, factors, sums, group_factor, shares, group_sum, my_factor, before_ref, factor_row,
    staged, arrived, keys_values,
    loads, small, send1, recv1, send2, recv2, send3, recv3, send6, recv6, send, recv,
    send4, recv4, send5, recv5,
):
    grp, seq = lax.axis_index("grp"), lax.axis_index("seq")
    barrier = pltpu.get_barrier_semaphore()
    for d in range(1, n_seq):
        pl.semaphore_signal(
            barrier, inc=1, device_id=(grp, lax.rem(seq + d, n_seq)), device_id_type=MESH
        )
    for d in range(1, n_grp):
        pl.semaphore_signal(
            barrier, inc=1, device_id=(lax.rem(grp + d, n_grp), seq), device_id_type=MESH
        )
    fetches = [
        pltpu.make_async_copy(src, dst, loads.at[i])
        for i, (src, dst) in enumerate(
            [
                (w_xz_hbm, w_xz_ref), (w_out_hbm, w_out_ref), (w_kv_hbm, w_kv_ref),
                (w_q_hbm, w_q_ref), (w_o_hbm, w_o_ref),
            ]
        )
    ]
    for fetch in fetches:
        fetch.start()
    place[...] = jnp.zeros_like(place)
    request_lists(n_seq, slots, owner_ref, block_ref, wanted, place)
    placing = pltpu.make_async_copy(place, place_here, small.at[0])
    placing.start()

    count = tokens_ref.shape[0]
    blocks = normed_ref.shape[0]
    chunks = count // CH
    spread = head_spread()
    row = lax.broadcasted_iota(jnp.int32, (CH, CH), 0)
    col = lax.broadcasted_iota(jnp.int32, (CH, CH), 1)
    lower = row >= col
    upto = (row <= col).astype(F32)
    first_lanes = lax.broadcasted_iota(jnp.int32, (CH, 128), 1) < P_SIZE
    bias, rate = column(bias_ref[...]), column(rate_ref[...])
    skip = dot_tn(split3(jnp.broadcast_to(column(skip_ref[...]), (H, 8))), spread)[0:1]

    carried[...] = jnp.zeros_like(carried)
    fetches[0].wait()

    def states(t, base):
        start = pl.multiple_of(t * 2 * CH, 2 * CH)
        tile = pl.ds(start, 2 * CH)
        normed = rms_rows(tokens_ref[tile], gain_ref[...])
        stream = dot(normed, w_xz_ref[:, :INNER]).astype(BF16)
        xz_ref[tile, :INNER] = stream
        xz_ref[tile, INNER:] = dot(normed, w_xz_ref[:, INNER:]).astype(BF16)
        maps = dot(normed, w_bc_ref[...]).astype(BF16)
        maps_ref[tile] = maps
        steps_t = jax.nn.softplus(dot_nt(w_dt_ref[...], normed) + bias)
        for i in range(2):
            c = t * 2 + i
            rows = slice(i * CH, (i + 1) * CH)
            u_t = steps_t[:, rows]
            decay_t = -(rate * u_t + jump_ref[c])
            run_t = jnp.dot(
                decay_t, upto, precision=lax.Precision.HIGHEST, preferred_element_type=F32
            )
            step_ref[c] = u_t
            run_ref[c] = run_t
            base_ref[c] = run_t + base
            ending = run_t[:, CH - 1 :]
            tail_t = jnp.exp(ending - run_t) * u_t
            tail_weight = dot_tn(split3(tail_t), spread)
            last = dot_tn(split3(jnp.broadcast_to(jnp.exp(ending), (H, 8))), spread)[0:1]
            state = carried[...]
            high = state.astype(BF16)
            state_ref[c, :NS] = high
            state_ref[c, NS:] = (state - high.astype(F32)).astype(BF16)
            tail = (tail_weight * stream[rows].astype(F32)).astype(BF16)
            carried[...] = last * state + dot_tn(maps[rows, :NS], tail)
            base = base + ending
        return base

    base = lax.fori_loop(0, chunks // 2, states, jnp.zeros((H, 1), F32))
    width = parts.shape[-1]
    spots = INNER // width
    for k in range(n_seq):
        down, across_lanes = k // spots, k % spots
        final[k] = carried[
            down * ROWS : (down + 1) * ROWS, across_lanes * width : (across_lanes + 1) * width
        ].astype(BF16)
    product = dot_tn(split3(jnp.broadcast_to(jnp.exp(base), (H, 8))), spread)[0:1]
    for i in range(8):
        total[i : i + 1, :] = product[:, i * 128 : (i + 1) * 128]

    def mix_block(c, carry):
        rows = pl.ds(pl.multiple_of(c * CH, CH), CH)
        run_t, u_t = run_ref[c], step_ref[c]
        run = jnp.concatenate([run_t, jnp.zeros((CH - H, CH), F32)], axis=0).T
        cmap = maps_ref[rows, NS:]
        crossing = dot_nt(cmap, maps_ref[rows, :NS])
        reach = dot_tn(split3(jnp.exp(run_t)), spread)
        reached = dot(jnp.concatenate([cmap, cmap], axis=1), state_ref[c])
        for p in range(PAIRS):
            lanes = slice(p * 128, (p + 1) * 128)
            x = xz_ref[rows, lanes]
            pieces = []
            for h in (2 * p, 2 * p + 1):
                gap = run[:, h : h + 1] - run_t[h : h + 1, :]
                weight = jnp.exp(jnp.where(lower, gap, -1e30))
                pieces.append((crossing * weight * u_t[h : h + 1, :]).astype(BF16))
            zero = jnp.zeros_like(x)
            stacked = jnp.concatenate(
                [jnp.where(first_lanes, x, zero), jnp.where(first_lanes, zero, x)], axis=0
            )
            pre_ref[rows, lanes] = (
                dot(jnp.concatenate(pieces, axis=1), stacked)
                + reach[:, lanes] * reached[:, lanes]
                + skip[:, lanes] * x.astype(F32)
            )
        return carry

    pl.semaphore_wait(barrier, n_seq + n_grp - 2)
    peers = [lax.rem(seq + d, n_seq) for d in range(n_seq)]
    layers = [lax.rem(grp + d, n_grp) for d in range(n_grp)]

    def across(src, dst, sender, receiver, d):
        return pltpu.make_async_remote_copy(
            src_ref=src, dst_ref=dst, send_sem=sender.at[d], recv_sem=receiver.at[d],
            device_id=(grp, peers[d]), device_id_type=MESH,
        )

    def along(src, dst, sender, receiver, d):
        return pltpu.make_async_remote_copy(
            src_ref=src, dst_ref=dst, send_sem=sender.at[d], recv_sem=receiver.at[d],
            device_id=(layers[d], seq), device_id_type=MESH,
        )

    first = []
    for d in range(1, n_seq):
        first.append(across(final.at[peers[d]], parts.at[seq], send1, recv1, d))
        first.append(across(total, factors.at[seq], send2, recv2, d))
    for copy in first:
        copy.start()
    asking = []
    for d in range(1, n_seq):
        asking.append(across(wanted.at[peers[d]], asked.at[seq], send3, recv3, d))
        asking[-1].start()
    parts[seq] = final[seq]
    factors[seq] = total[...]
    asked[seq] = wanted[seq]

    lax.fori_loop(0, chunks // 2, mix_block, 0)
    for copy in first:
        copy.wait()
    lanes_here = pl.ds(pl.multiple_of(lax.rem(seq, spots) * width, width), width)

    def row_of(tile):
        for i in range(8):
            factor_row[:, i * 128 : (i + 1) * 128] = tile[i : i + 1, :]
        return factor_row[:, lanes_here]

    running = jnp.zeros((ROWS, width), F32)
    product = jnp.ones((8, 128), F32)
    for k in range(n_seq):
        sums[k] = running
        group_factor[k] = product
        running = row_of(factors[k]) * running + parts[k].astype(F32)
        product = product * factors[k]
    group_sum[grp] = running.astype(BF16)
    my_factor[grp] = product
    second = []
    for d in range(1, n_grp):
        second.append(along(group_sum.at[grp], group_sum.at[grp], send4, recv4, d))
        second.append(along(my_factor.at[grp], my_factor.at[grp], send5, recv5, d))
    for copy in second:
        copy.start()
    for copy in asking:
        copy.wait()
    listing = pltpu.make_async_copy(asked, asked_here, small.at[1])
    listing.start()
    lax.fori_loop(chunks // 2, 3 * chunks // 4, mix_block, 0)
    for copy in second:
        copy.wait()
    carry = jnp.zeros((ROWS, width), F32)
    for g in range(n_grp):
        new = row_of(my_factor[g]) * carry + group_sum[g].astype(F32)
        carry = jnp.where(g < grp, new, carry)
    for k in range(n_seq):
        shares[k] = (sums[k] + row_of(group_factor[k]) * carry).astype(BF16)
    third = []
    for d in range(1, n_seq):
        third.append(across(shares.at[peers[d]], before_ref.at[seq], send6, recv6, d))
        third[-1].start()
    before_ref[seq] = shares[seq]
    lax.fori_loop(3 * chunks // 4, chunks, mix_block, 0)
    for copy in third:
        copy.wait()
    listing.wait()
    placing.wait()
    for fetch in fetches[1:]:
        fetch.wait()

    group = lax.broadcasted_iota(jnp.int32, (256, 256), 0) // P_SIZE
    other = lax.broadcasted_iota(jnp.int32, (256, 256), 1) // P_SIZE
    same = (group == other).astype(BF16)

    def finish(t, carry):
        tile = pl.ds(pl.multiple_of(t * 2 * CH, 2 * CH), 2 * CH)
        before = jnp.concatenate(
            [
                jnp.concatenate([before_ref[a * spots + b] for b in range(spots)], axis=1)
                for a in range(NS // ROWS)
            ],
            axis=0,
        )
        entered = dot(maps_ref[tile, NS:], before)
        reach = jnp.concatenate(
            [dot_tn(split3(jnp.exp(base_ref[t * 2 + i])), spread) for i in range(2)], axis=0
        )
        mixed = pre_ref[tile] + reach * entered
        gate = xz_ref[tile, INNER:].astype(F32)
        gated = mixed * (gate * jax.nn.sigmoid(gate))
        squares = (gated * gated).astype(BF16)
        power = jnp.concatenate(
            [dot(squares[:, i * 256 : (i + 1) * 256], same) for i in range(INNER // 256)], axis=1
        )
        scaled = (gated * lax.rsqrt(power * (1.0 / P_SIZE) + EPS) * gain2_ref[...]).astype(BF16)
        middle = (tokens_ref[tile].astype(F32) + dot(scaled, w_out_ref[...])).astype(BF16)
        mid_ref[tile] = middle
        normed_ref[pl.ds(t * 4, 4)] = rms_rows(middle, gain3_ref[...]).reshape(4, BL, 512)
        return carry

    lax.fori_loop(0, chunks // 2, finish, 0)
    copies = []
    for d in range(1, n_seq):
        for j in range(slots):
            staged[d, j] = normed_ref[asked_here[peers[d], j, 0]]
        copies.append(across(staged.at[d], arrived.at[seq], send, recv, d))
        copies[-1].start()
    group = 4
    quarter = lax.broadcasted_iota(jnp.int32, (BL, 256), 1) // P_SIZE

    def own_blocks(t, carry):
        rows = normed_ref[pl.ds(t * group, group)].reshape(group * BL, 512)
        keys_values[pl.ds(t * group, group)] = (
            dot(rows, w_kv_ref[...]).astype(BF16).reshape(group, BL, 2 * INNER)
        )
        asking = (
            dot(rows, w_q_ref[...]).astype(BF16).astype(F32) * (1.0 / math.sqrt(P_SIZE))
        ).astype(BF16)
        queries[pl.ds(t * group, group)] = asking.reshape(group, BL, INNER)
        return carry

    lax.fori_loop(0, blocks // group, own_blocks, 0)
    for j in range(slots):
        keys_values[blocks + seq * slots + j] = keys_values[asked_here[seq, j, 0]]
    for d in range(1, n_seq):
        origin = lax.rem(seq + n_seq - d, n_seq)
        copies[d - 1].wait_recv()
        rows = arrived[origin].reshape(slots * BL, 512)
        keys_values[pl.ds(blocks + origin * slots, slots)] = (
            dot(rows, w_kv_ref[...]).astype(BF16).reshape(slots, BL, 2 * INNER)
        )

    first_half = lax.broadcasted_iota(jnp.int32, (BL, 128), 1) < P_SIZE

    def attend(t, carry):
        units = [(i, u) for i in range(PAIRED) for u in range(QUADS)]
        spots = [
            [t * PAIRED + i]
            + [blocks + place_here[k, t * PAIRED + i] for k in range(KN)]
            for i in range(PAIRED)
        ]

        def score(n):
            i, u = units[n]
            keys = jnp.concatenate(
                [keys_values[spot, :, u * 256 : (u + 1) * 256] for spot in spots[i]], axis=0
            )
            q = queries[t * PAIRED + i, :, u * 256 : (u + 1) * 256]
            zero = jnp.zeros_like(q)
            q = jnp.concatenate([jnp.where(quarter == h, q, zero) for h in range(4)], axis=0)
            scores[n] = dot_nt(keys, q)

        def mix(n):
            i, u = units[n]
            for half in range(2):
                lanes = slice(u * 256 + half * 128, u * 256 + (half + 1) * 128)
                values = slice(INNER + lanes.start, INNER + lanes.stop)
                part = scores[n, :, half * 128 : (half + 1) * 128]
                raised = jnp.exp(part - jnp.max(part, axis=0, keepdims=True))
                weight = raised * (1.0 / jnp.sum(raised, axis=0, keepdims=True))
                value = jnp.concatenate(
                    [keys_values[spot, :, values] for spot in spots[i]], axis=0
                )
                mixed = dot_tn(weight.astype(BF16), value)
                xz_ref[pl.ds((t * PAIRED + i) * BL, BL), lanes] = jnp.where(
                    first_half, mixed[:BL], mixed[BL:]
                ).astype(BF16)

        ahead = 3
        for n in range(len(units) + ahead):
            if n < len(units):
                score(n)
            if n >= ahead:
                mix(n - ahead)
        return carry

    lax.fori_loop(0, blocks // PAIRED, attend, 0)

    def project(t, carry):
        rows = pl.ds(t * 256, 256)
        out_ref[rows] = (
            mid_ref[rows].astype(F32) + dot(xz_ref[rows, :INNER], w_o_ref[...])
        ).astype(BF16)
        return carry

    lax.fori_loop(0, blocks * BL // 256, project, 0)
    for copy in copies:
        copy.wait_send()


def layer_part(
    n_grp, n_seq, tokens, norm_gain1, w_xz, w_bc, w_dt, dt_bias, decay_rate, curve_jump,
    skip_gain, norm_gain2, w_out, norm_gain3, w_q, w_kv, w_o, nbr_owner, nbr_block,
):
    count = tokens.shape[0]
    blocks, chunks = count // BL, count // CH
    slots = max(2, -(-blocks * KN // n_seq))
    width = INNER // (n_seq // 8)
    vmem = pl.BlockSpec(memory_space=pltpu.VMEM)
    anywhere = pl.BlockSpec(memory_space=pl.ANY)
    dma = pltpu.SemaphoreType.DMA
    held = [
        (w_xz.shape, BF16), (w_out.shape, BF16), (w_q.shape, BF16), (w_kv.shape, BF16),
        (w_o.shape, BF16),
        ((count, 2 * INNER), BF16), ((count, 2 * NS), BF16), ((count, INNER), F32),
        ((chunks, 2 * NS, INNER), BF16), ((chunks, H, CH), F32), ((chunks, H, CH), F32),
        ((chunks, H, CH), F32), ((NS, INNER), F32),
        ((count, 512), BF16), ((blocks, BL, 512), BF16), ((blocks, BL, INNER), BF16),
        ((PAIRED * QUADS, SPAN, 256), F32),
        ((n_seq, ROWS, width), BF16), ((8, 128), F32), ((n_seq, 8, 128), jnp.int32),
        ((n_seq, 8, 128), jnp.int32), None, ((8, 128), jnp.int32), None,
        ((n_seq, ROWS, width), BF16), ((n_seq, 8, 128), F32), ((n_seq, ROWS, width), F32),
        ((n_seq, 8, 128), F32), ((n_seq, ROWS, width), BF16), ((n_grp, ROWS, width), BF16),
        ((n_grp, 8, 128), F32), ((n_seq, ROWS, width), BF16), ((1, INNER), F32),
        ((n_seq, slots, BL, 512), BF16), ((n_seq, slots, BL, 512), BF16),
        ((blocks + n_seq * slots, BL, 2 * INNER), BF16),
    ]
    scratch = [pltpu.VMEM(*item) if item else None for item in held]
    scratch[21] = pltpu.SMEM((n_seq, 8, 128), jnp.int32)
    scratch[23] = pltpu.SMEM((8, 128), jnp.int32)
    return pl.pallas_call(
        functools.partial(layer_kernel, n_grp, n_seq, slots),
        in_specs=[vmem] * 12 + [anywhere] * 5,
        out_specs=vmem,
        out_shape=jax.ShapeDtypeStruct((count, 512), BF16),
        scratch_shapes=scratch
        + [dma((5,)), dma((2,))]
        + [dma((n_seq,))] * 10
        + [dma((n_grp,))] * 4,
        compiler_params=pltpu.CompilerParams(
            collective_id=0, has_side_effects=True, vmem_limit_bytes=VMEM_LIMIT
        ),
        name="layer_part",
    )(
        tokens, norm_gain1[None], w_bc, w_dt.T, dt_bias[None], decay_rate[None],
        curve_jump.reshape(chunks, 1, CH), skip_gain[None], norm_gain2[None], norm_gain3[None],
        nbr_owner.T, nbr_block.T, w_xz, w_out, w_q, w_kv, w_o,
    )


def solution(mesh):
    shard = P(("grp", "seq"), None)
    in_specs = (
        shard, P(), P(), P(), P(), P(), P(), P(("grp", "seq")), P(), P(), P(), P(), P(), P(),
        P(), shard, shard,
    )
    body = functools.partial(layer_part, mesh.shape["grp"], mesh.shape["seq"])
    return jax.shard_map(body, mesh=mesh, in_specs=in_specs, out_specs=shard, check_vma=False)
```

time: 94.9 us -> 75.5 us (0.80)
  Pallas kernels: 89.8 us -> 73 us
  local copies, waits for them, and re-layouts: 4.48 us -> 2.26 us
    pallas_call x4 -> x1, Pallas kernels: 89.8 us -> 73 us  [layer_part(): pl.pallas_call(functools.partial(layer_kernel, n_grp, n_seq, slots), in_s...]
    unnamed x3 -> x1, local copies, waits for them, and re-layouts: 2.27 us -> 2.26 us
where the time goes in v2:
time: 75.5 us; the launch traced here: 75.3 us
  Pallas kernels  73 us (97%)
  local copies, waits for them, and re-layouts  2.26 us (3%)
    pallas_call x1, Pallas kernels, layer_part(): pl.pallas_call(functools.partial(layer_kernel, n_grp, n_seq, slots), in_s...  73 us
    unnamed x1, local copies, waits for them, and re-layouts  2.26 us

profile of v2, /device:TPU:1, one launch (start us, length us, event | category | flops | bytes accessed | tf_op | source)
XLA Modules:
  0.0 75.3 jit_solution(10511333609406081845)
XLA Ops:
  0.0 73.0 %layer_part.1 = bf16[1024,512]{1,0:T(8,128)(2,1)} custom-call(bf16[1024,512]{1,0:T(8,128)(2,1)} %tokens_ref.1, f32[1,512]{1,0:T(1,128)} %bitcast.13, bf16[512,256]{1,0:T(8,128)(2,1)} %w_bc_ref.1, bf16[16,512]{1,0:T(8,128)(2,1)} %bitcast.10, f32[1,16]{1,0:T(1,128)} %bitcast.17, f32[1,16]{1,0:T(1,128)} %bitcast.18, f32[8,1,128]{2,1,0:T(1,128)} %bitcast.11, ...), custom_call_target="tpu_custom_call" | custom-call | tf_op jit(solution)/shard_map/layer_part/pallas_call | solution.py:463
  73.0 2.3 %copy.19 = bf16[1024,512]{1,0:T(8,128)(2,1)} copy(bf16[1024,512]{1,0:T(8,128)(2,1)} %layer_part.1) | data formatting | bytes 2097152

commit v3 on v2

--- a/solution.py
+++ b/solution.py
@@ -21,7 +21,7 @@
 QUADS = INNER // 256
 PAIRED = 2
 EPS = 1e-05
-VMEM_LIMIT = 60 * 1024 * 1024
+VMEM_LIMIT = 62 * 1024 * 1024
 MESH = pl.DeviceIdType.MESH
 F32 = jnp.float32
 BF16 = jnp.bfloat16
@@ -110,7 +110,7 @@
     xz_ref, maps_ref, pre_ref, state_ref, step_ref, run_ref, base_ref, carried,
     mid_ref, normed_ref, queries, scores,
     final, total, wanted, asked, asked_here, place, place_here,
-    parts, factors, sums, group_factor, shares, group_sum, my_factor, before_ref, factor_row,
+    parts, factors, sums, group_factor, group_sum, my_factor, before_ref, factor_row,
     staged, arrived, keys_values,
     loads, small, send1, recv1, send2, recv2, send3, recv3, send6, recv6, send, recv,
     send4, recv4, send5, recv5,
@@ -206,6 +206,9 @@
         rows = pl.ds(pl.multiple_of(c * CH, CH), CH)
         run_t, u_t = run_ref[c], step_ref[c]
         run = jnp.concatenate([run_t, jnp.zeros((CH - H, CH), F32)], axis=0).T
+        scores[c, :CH, :CH] = jnp.concatenate(
+            [jnp.exp(base_ref[c]), jnp.zeros((CH - H, CH), F32)], axis=0
+        ).T
         cmap = maps_ref[rows, NS:]
         crossing = dot_nt(cmap, maps_ref[rows, :NS])
         reach = dot_tn(split3(jnp.exp(run_t)), spread)
@@ -259,7 +262,7 @@
     factors[seq] = total[...]
     asked[seq] = wanted[seq]
 
-    lax.fori_loop(0, chunks // 2, mix_block, 0)
+    lax.fori_loop(0, 3 * chunks // 8, mix_block, 0)
     for copy in first:
         copy.wait()
     lanes_here = pl.ds(pl.multiple_of(lax.rem(seq, spots) * width, width), width)
@@ -288,7 +291,7 @@
         copy.wait()
     listing = pltpu.make_async_copy(asked, asked_here, small.at[1])
     listing.start()
-    lax.fori_loop(chunks // 2, 3 * chunks // 4, mix_block, 0)
+    lax.fori_loop(3 * chunks // 8, 5 * chunks // 8, mix_block, 0)
     for copy in second:
         copy.wait()
     carry = jnp.zeros((ROWS, width), F32)
@@ -296,13 +299,13 @@
         new = row_of(my_factor[g]) * carry + group_sum[g].astype(F32)
         carry = jnp.where(g < grp, new, carry)
     for k in range(n_seq):
-        shares[k] = (sums[k] + row_of(group_factor[k]) * carry).astype(BF16)
+        final[k] = (sums[k] + row_of(group_factor[k]) * carry).astype(BF16)
     third = []
     for d in range(1, n_seq):
-        third.append(across(shares.at[peers[d]], before_ref.at[seq], send6, recv6, d))
+        third.append(across(final.at[peers[d]], before_ref.at[seq], send6, recv6, d))
         third[-1].start()
-    before_ref[seq] = shares[seq]
-    lax.fori_loop(3 * chunks // 4, chunks, mix_block, 0)
+    before_ref[seq] = final[seq]
+    lax.fori_loop(5 * chunks // 8, chunks, mix_block, 0)
     for copy in third:
         copy.wait()
     listing.wait()
@@ -314,39 +317,64 @@
     other = lax.broadcasted_iota(jnp.int32, (256, 256), 1) // P_SIZE
     same = (group == other).astype(BF16)
 
-    def finish(t, carry):
-        tile = pl.ds(pl.multiple_of(t * 2 * CH, 2 * CH), 2 * CH)
-        before = jnp.concatenate(
+    before = jnp.concatenate(
+        [
+            jnp.concatenate([before_ref[a * spots + b] for b in range(spots)], axis=1)
+            for a in range(NS // ROWS)
+        ],
+        axis=0,
+    )
+    padded = jnp.concatenate([spread[:H], jnp.zeros((128 - H, INNER), BF16)], axis=0)
+    padded = jnp.concatenate([padded, padded], axis=0)
+    copies = []
+    for q in range(BL // ROWS):
+        within = slice(q * ROWS, (q + 1) * ROWS)
+
+        def strip(ref, lanes):
+            return jnp.concatenate(
+                [ref[b * BL + q * ROWS : b * BL + (q + 1) * ROWS, lanes] for b in range(blocks)],
+                axis=0,
+            )
+
+        entered = dot(strip(maps_ref, slice(NS, 2 * NS)), before)
+        reach = jnp.concatenate(
             [
-                jnp.concatenate([before_ref[a * spots + b] for b in range(spots)], axis=1)
-                for a in range(NS // ROWS)
+                scores[b // 2, b % 2 * BL + q * ROWS : b % 2 * BL + (q + 1) * ROWS, :128]
+                for b in range(blocks)
             ],
             axis=0,
         )
-        entered = dot(maps_ref[tile, NS:], before)
-        reach = jnp.concatenate(
-            [dot_tn(split3(jnp.exp(base_ref[t * 2 + i])), spread) for i in range(2)], axis=0
-        )
-        mixed = pre_ref[tile] + reach * entered
-        gate = xz_ref[tile, INNER:].astype(F32)
+        high = reach.astype(BF16)
+        low = (reach - high.astype(F32)).astype(BF16)
+        reach = dot(jnp.concatenate([high, low], axis=1), padded)
+        mixed = strip(pre_ref, slice(0, INNER)) + reach * entered
+        gate = strip(xz_ref, slice(INNER, 2 * INNER)).astype(F32)
         gated = mixed * (gate * jax.nn.sigmoid(gate))
         squares = (gated * gated).astype(BF16)
         power = jnp.concatenate(
             [dot(squares[:, i * 256 : (i + 1) * 256], same) for i in range(INNER // 256)], axis=1
         )
         scaled = (gated * lax.rsqrt(power * (1.0 / P_SIZE) + EPS) * gain2_ref[...]).astype(BF16)
-        middle = (tokens_ref[tile].astype(F32) + dot(scaled, w_out_ref[...])).astype(BF16)
-        mid_ref[tile] = middle
-        normed_ref[pl.ds(t * 4, 4)] = rms_rows(middle, gain3_ref[...]).reshape(4, BL, 512)
-        return carry
-
-    lax.fori_loop(0, chunks // 2, finish, 0)
-    copies = []
-    for d in range(1, n_seq):
+        middle = strip(tokens_ref, slice(0, 512)).astype(F32) + dot(scaled, w_out_ref[...])
+        middle = middle.astype(BF16)
+        for b in range(blocks):
+            mid_ref[b * BL + q * ROWS : b * BL + (q + 1) * ROWS] = middle[
+                b * ROWS : (b + 1) * ROWS
+            ]
+        normed_ref[:, within] = rms_rows(middle, gain3_ref[...]).reshape(blocks, ROWS, 512)
+        for d in range(1, n_seq):
+            for j in range(slots):
+                staged[q, d, j] = normed_ref[asked_here[peers[d], j, 0], within]
+            copies.append(
+                pltpu.make_async_remote_copy(
+                    src_ref=staged.at[q, d], dst_ref=arrived.at[q, seq],
+                    send_sem=send.at[q, d], recv_sem=recv.at[q, d],
+                    device_id=(grp, peers[d]), device_id_type=MESH,
+                )
+            )
+            copies[-1].start()
         for j in range(slots):
-            staged[d, j] = normed_ref[asked_here[peers[d], j, 0]]
-        copies.append(across(staged.at[d], arrived.at[seq], send, recv, d))
-        copies[-1].start()
+            arrived[q, seq, j] = normed_ref[asked_here[seq, j, 0], within]
     group = 4
     quarter = lax.broadcasted_iota(jnp.int32, (BL, 256), 1) // P_SIZE
 
@@ -362,15 +390,15 @@
         return carry
 
     lax.fori_loop(0, blocks // group, own_blocks, 0)
-    for j in range(slots):
-        keys_values[blocks + seq * slots + j] = keys_values[asked_here[seq, j, 0]]
-    for d in range(1, n_seq):
-        origin = lax.rem(seq + n_seq - d, n_seq)
-        copies[d - 1].wait_recv()
-        rows = arrived[origin].reshape(slots * BL, 512)
-        keys_values[pl.ds(blocks + origin * slots, slots)] = (
-            dot(rows, w_kv_ref[...]).astype(BF16).reshape(slots, BL, 2 * INNER)
-        )
+    for q in range(BL // ROWS):
+        for d in range(1, n_seq):
+            copies[q * (n_seq - 1) + d - 1].wait_recv()
+        several = 16 // slots
+        for part in range(n_seq // several):
+            rows = arrived[q, part * several : (part + 1) * several].reshape(16 * ROWS, 512)
+            keys_values[
+                blocks + part * 16 : blocks + (part + 1) * 16, q * ROWS : (q + 1) * ROWS
+            ] = dot(rows, w_kv_ref[...]).astype(BF16).reshape(16, ROWS, 2 * INNER)
 
     first_half = lax.broadcasted_iota(jnp.int32, (BL, 128), 1) < P_SIZE
 
@@ -452,9 +480,10 @@
         ((n_seq, ROWS, width), BF16), ((8, 128), F32), ((n_seq, 8, 128), jnp.int32),
         ((n_seq, 8, 128), jnp.int32), None, ((8, 128), jnp.int32), None,
         ((n_seq, ROWS, width), BF16), ((n_seq, 8, 128), F32), ((n_seq, ROWS, width), F32),
-        ((n_seq, 8, 128), F32), ((n_seq, ROWS, width), BF16), ((n_grp, ROWS, width), BF16),
+        ((n_seq, 8, 128), F32), ((n_grp, ROWS, width), BF16),
         ((n_grp, 8, 128), F32), ((n_seq, ROWS, width), BF16), ((1, INNER), F32),
-        ((n_seq, slots, BL, 512), BF16), ((n_seq, slots, BL, 512), BF16),
+        ((BL // ROWS, n_seq, slots, ROWS, 512), BF16),
+        ((BL // ROWS, n_seq, slots, ROWS, 512), BF16),
         ((blocks + n_seq * slots, BL, 2 * INNER), BF16),
     ]
     scratch = [pltpu.VMEM(*item) if item else None for item in held]
@@ -467,7 +496,8 @@
         out_shape=jax.ShapeDtypeStruct((count, 512), BF16),
         scratch_shapes=scratch
         + [dma((5,)), dma((2,))]
-        + [dma((n_seq,))] * 10
+        + [dma((n_seq,))] * 8
+        + [dma((BL // ROWS, n_seq))] * 2
         + [dma((n_grp,))] * 4,
         compiler_params=pltpu.CompilerParams(
             collective_id=0, has_side_effects=True, vmem_limit_bytes=VMEM_LIMIT

time: 75.5 us -> 72.2 us (0.956)
  Pallas kernels: 73 us -> 69.7 us
    pallas_call x1, Pallas kernels: 73 us -> 69.7 us  [layer_part(): pl.pallas_call(functools.partial(layer_kernel, n_grp, n_seq, slots), in_s...]
where the time goes in v3:
time: 72.2 us; the launch traced here: 72 us
  Pallas kernels  69.7 us (97%)
  local copies, waits for them, and re-layouts  2.26 us (3%)
    pallas_call x1, Pallas kernels, layer_part(): pl.pallas_call(functools.partial(layer_kernel, n_grp, n_seq, slots), in_s...  69.7 us
    unnamed x1, local copies, waits for them, and re-layouts  2.26 us

profile of v3, /device:TPU:1, one launch (start us, length us, event | category | flops | bytes accessed | tf_op | source)
XLA Modules:
  0.0 72.0 jit_solution(10562163566091585823)
XLA Ops:
  0.0 69.7 %layer_part.1 = bf16[1024,512]{1,0:T(8,128)(2,1)} custom-call(bf16[1024,512]{1,0:T(8,128)(2,1)} %tokens_ref.1, f32[1,512]{1,0:T(1,128)} %bitcast.13, bf16[512,256]{1,0:T(8,128)(2,1)} %w_bc_ref.1, bf16[16,512]{1,0:T(8,128)(2,1)} %bitcast.10, f32[1,16]{1,0:T(1,128)} %bitcast.17, f32[1,16]{1,0:T(1,128)} %bitcast.18, f32[8,1,128]{2,1,0:T(1,128)} %bitcast.11, ...), custom_call_target="tpu_custom_call" | custom-call | tf_op jit(solution)/shard_map/layer_part/pallas_call | solution.py:492
  69.7 2.3 %copy.19 = bf16[1024,512]{1,0:T(8,128)(2,1)} copy(bf16[1024,512]{1,0:T(8,128)(2,1)} %layer_part.1) | data formatting | bytes 2097152
